TPU v7x, 128 devices: a whole 4x4x4 slice. The times are simulated.
128 devices in a mesh: req: 4 (over z_hi, core), ctx: 32 (over x, y, z_lo).
Axes of the slice: x: 4, y: 4, z: 4 (z_hi: 2, z_lo: 2; z = z_hi * 2 + z_lo), core: 2. Of those that a mesh axis runs over, the one named last changes fastest.
Arguments:
- queries: bfloat16 [4, 4096, 8192], P('req', 'ctx'), may hold values from -30 to 30
- stretch_kv: bfloat16 [4, 4096, 2048], P('req', 'ctx'), may hold values from -13 to 13
- page_pool: bfloat16 [256, 16, 2048], P(('req', 'ctx')), may hold values from -6 to 6
- slot_owner: int32 [256], replicated, may hold values from 0 to 3, as said below
- slot_fill: int32 [256], replicated, may hold values from 1 to 16
Outputs:
- attended: bfloat16 [4, 4096, 8192], P('req', 'ctx')
Inputs may be any that keep to these rules, and one draw needn't show every extreme that they name: `slot_owner`: store device s (numbered along req, then ctx) holds slots s * 2 to s * 2 + 1; they hold 1 pages each of two different requests. In every draw all store devices of some ctx index hold pages of the same two requests.
All inputs are finite; a program needn't handle non-finite values.
Results may differ from a plain program's by a relative error of at most 0.0095.
Values may be sent and summed in bfloat16 or wider, within the bound.
A program may use at most 192 MiB of HBM per device.

v0:
```python
import math

import jax
import jax.numpy as jnp
from jax import lax
from jax.sharding import PartitionSpec as P

HEADS = 64
KV_HEADS = 8
HEAD_DIM = 128


masked_score = -1e30


def update(carry_in, query_heads, key_block, keep_block):
    running_max, running_sum, summed = carry_in
    half_width = key_block.shape[1] // 2
    row_count = key_block.shape[0]
    key_rows = key_block[:, :half_width].reshape(row_count, KV_HEADS, HEAD_DIM)
    values = key_block[:, half_width:].reshape(row_count, KV_HEADS, HEAD_DIM)
    scores = jnp.einsum(
        "tkgd,jkd->kgtj", query_heads, key_rows, preferred_element_type=jnp.float32
    ) * HEAD_DIM ** (-0.5)
    allowed = keep_block[None, None]
    scores = jnp.where(allowed, scores, masked_score)
    new_max = jnp.maximum(running_max, jnp.max(scores, axis=-1))
    weights = jnp.where(allowed, jnp.exp(scores - new_max[..., None]), 0.0).astype(jnp.bfloat16)
    factor = jnp.exp(running_max - new_max)
    running_sum = running_sum * factor + jnp.sum(weights, axis=-1, dtype=jnp.float32)
    summed = summed * factor[..., None] + jnp.einsum(
        "kgtj,jkd->kgtd", weights, values, preferred_element_type=jnp.float32
    )
    return (new_max, running_sum, summed)


def absorb(carry_in, query_heads, rows_kv, visible):
    row_count = rows_kv.shape[0]
    block_rows = math.gcd(row_count, 512)

    def step(block_index, carry_now):
        key_block = lax.dynamic_slice_in_dim(rows_kv, block_index * block_rows, block_rows, 0)
        keep_block = lax.dynamic_slice_in_dim(visible, block_index * block_rows, block_rows, 1)
        return update(carry_now, query_heads, key_block, keep_block)

    return lax.fori_loop(0, row_count // block_rows, step, carry_in)


def combine_states(first_state, second):
    joint_max = jnp.maximum(first_state[0], second[0])
    left_scale = jnp.exp(first_state[0] - joint_max)
    right_scale = jnp.exp(second[0] - joint_max)
    joint_sum = first_state[1] * left_scale + second[1] * right_scale
    joint_acc = first_state[2] * left_scale[..., None] + second[2] * right_scale[..., None]
    return (joint_max, joint_sum, joint_acc)


def make_state(group_size, query_count):
    return (
        jnp.full((KV_HEADS, group_size, query_count), masked_score, jnp.float32),
        jnp.zeros((KV_HEADS, group_size, query_count), jnp.float32),
        jnp.zeros((KV_HEADS, group_size, query_count, HEAD_DIM), jnp.float32),
    )


def choose_slots(owners, target):
    matches = owners == target
    rank_of = jnp.cumsum(matches.astype(jnp.int32), axis=-1) - 1
    places = jnp.arange(owners.shape[-1], dtype=jnp.int32)
    matched = matches & (rank_of == 0)
    picked = [jnp.sum(jnp.where(matched, places, 0), axis=-1)]
    present = [jnp.any(matched, axis=-1)]
    return (jnp.stack(picked, axis=-1), jnp.stack(present, axis=-1))


def shards(queries, stretch_kv, page_pool, slot_owner, slot_fill):
    ctx_size = lax.axis_size("ctx")
    req_size = lax.axis_size("req")
    req_index = lax.axis_index("req")
    ctx_index = lax.axis_index("ctx")
    query_count = queries.shape[1]
    group_size = HEADS // KV_HEADS
    local_rows = queries[0]
    query_heads = local_rows.reshape(query_count, KV_HEADS, group_size, HEAD_DIM)
    kv_width = page_pool.shape[-1]
    slots_dev = page_pool.shape[0]
    page_len = page_pool.shape[1]
    owners = slot_owner.reshape(-1, slots_dev)
    fill_table = slot_fill.reshape(-1, slots_dev)
    within = jnp.arange(page_len, dtype=jnp.int32)
    initial = make_state(group_size, query_count)
    own_slots = lax.dynamic_index_in_dim(
        owners, req_index * ctx_size + ctx_index, 0, keepdims=False
    )
    targets = jnp.arange(req_size, dtype=jnp.int32)[:, None]
    picked, present = choose_slots(own_slots[None, :], targets)
    per_request = jnp.where(present[..., None, None], page_pool[picked], 0)
    arrived = lax.all_to_all(per_request, "req", split_axis=0, concat_axis=0, tiled=True)
    sources = lax.dynamic_index_in_dim(
        owners.reshape(req_size, ctx_size, slots_dev), ctx_index, 1, keepdims=False
    )
    source_fill = lax.dynamic_index_in_dim(
        fill_table.reshape(req_size, ctx_size, slots_dev), ctx_index, 1, keepdims=False
    )
    chosen, alive_src = choose_slots(sources, req_index)
    counts = jnp.where(alive_src, jnp.take_along_axis(source_fill, chosen, axis=-1), 0)
    usable = (within[None, None, :] < counts[..., None]).astype(jnp.bfloat16).reshape(-1)
    tokens = arrived.reshape(-1, kv_width)
    prefix_state = absorb(
        initial,
        query_heads,
        lax.all_gather(tokens, "ctx", axis=0, tiled=True),
        (lax.all_gather(usable, "ctx", axis=0, tiled=True) > 0)[None, :],
    )
    first_query = ctx_index * query_count
    query_pos = first_query + jnp.arange(query_count, dtype=jnp.int32)
    key_piece = lax.all_gather(stretch_kv[0], "ctx", axis=0, tiled=True)
    key_pos = jnp.arange(key_piece.shape[0], dtype=jnp.int32)
    visible = key_pos[None, :] <= query_pos[:, None]
    stretch_result = lax.cond(
        jnp.int32(0) > first_query + query_count - 1,
        lambda carry_now: carry_now,
        lambda carry_now: absorb(carry_now, query_heads, key_piece, visible),
        initial,
    )
    joint_max, joint_sum, joint_acc = combine_states(prefix_state, stretch_result)
    result = (joint_acc / joint_sum[..., None]).astype(jnp.bfloat16)
    result_rows = result.transpose(2, 0, 1, 3).reshape(query_count, -1)
    return result_rows[None]


def solution(mesh):
    placed = (P("req", "ctx", None), P("req", "ctx", None), P(("req", "ctx"), None, None), P(), P())
    return jax.shard_map(
        shards, mesh=mesh, in_specs=placed, out_specs=P("req", "ctx", None), check_vma=False
    )
```

profile of v0, /device:TPU:2, one launch (start us, length us, event | category | flops | bytes accessed | tf_op | source)
XLA Modules:
  0.0 891.2 jit_solution(14111070831342279452)
XLA Ops:
  8.7 12.6 %all_to_all.5 = bf16[4,1,16,2048]{3,2,1,0:T(8,128)(2,1)} all-to-all(bf16[4,1,16,2048]{3,2,1,0:T(8,128)(2,1)S(1)} %bitcast_select_fusion.1), channel_id=1, replica_groups=mesh['req'=4,'ctx'=32] {'req'}, dimensions={0} | all-to-all | bytes 524288 | tf_op jit(solution)/shard_map/all_to_all | solution.py:98
  29.8 71.5 %all-reduce = bf16[2048]{0:T(1024)(128)(2,1)S(1)} all-reduce(bf16[2048]{0:T(1024)(128)(2,1)S(1)} %dynamic-update-slice), channel_id=1, replica_groups=mesh['req'=4,'ctx'=32] {'ctx'}, use_global_device_ids=true, to_apply=%add | all-reduce | flops 2048 | bytes 8192
  104.4 106.7 %all-gather.4.cloned.1.call-done = bf16[2048,2048]{1,0:T(8,128)(2,1)} async-done(((bf16[64,2048]{1,0:T(8,128)(2,1)}), bf16[2048,2048]{1,0:T(8,128)(2,1)}) %all-gather.4.cloned.1.call-update) | async-done | bytes 8388624 | tf_op jit(solution)/shard_map/all_gather | solution.py:112
  211.1 133.7 %while.36 = (s32[]{:T(128)}, f32[8,8,128]{2,1,0:T(8,128)S(1)}, f32[8,8,128]{2,1,0:T(8,128)S(1)}, f32[8,8,128,128]{3,2,1,0:T(8,128)}, pred[1,2048]{1,0:T(4,128)(4...) while((s32[]{:T(128)}, f32[8,8,128]{2,1,0:T(8,128)S(1)}, ...), condition=%wide.region_9.10_spmd.clone, body=%wide.region_6.9_spmd.clone.sunk | while | flops 2192613376 | bytes 71796936 | solution.py:46
  223.6 11.8 %convert_reduce_fusion.4 = (f32[8,8,128]{2,1,0:T(8,128)S(1)}, bf16[8,8,128,512]{2,3,1,0:T(8,128)(2,1)}) fusion(f32[8,8,128]{2,1,0:T(8,128)S(1)} %select_maximum_fusion.4, f32[8,512,128,8]{2,1,3,0:T(8,128)} %get-tuple-element.516, pred[512]{0:T(512)(128)(4,1)S(1)} %dynamic-slice_reduce_fusion.2), kind=kLoop, calls=%fused_computation.21.clone.1 | loop fusion | flops 29351936 | bytes 25231872 | tf_op jit(solution)/shard_map/while/body/eval_jaxpr/reduce_sum | solution.py:30
  256.4 11.8 %convert_reduce_fusion.4 = (f32[8,8,128]{2,1,0:T(8,128)S(1)}, bf16[8,8,128,512]{2,3,1,0:T(8,128)(2,1)}) fusion(f32[8,8,128]{2,1,0:T(8,128)S(1)} %select_maximum_fusion.4, f32[8,512,128,8]{2,1,3,0:T(8,128)} %get-tuple-element.516, pred[512]{0:T(512)(128)(4,1)S(1)} %dynamic-slice_reduce_fusion.2), kind=kLoop, calls=%fused_computation.21.clone.1 | loop fusion | flops 29351936 | bytes 25231872 | tf_op jit(solution)/shard_map/while/body/eval_jaxpr/reduce_sum | solution.py:30
  290.0 11.7 %convert_reduce_fusion.4 = (f32[8,8,128]{2,1,0:T(8,128)S(1)}, bf16[8,8,128,512]{2,3,1,0:T(8,128)(2,1)}) fusion(f32[8,8,128]{2,1,0:T(8,128)S(1)} %select_maximum_fusion.4, f32[8,512,128,8]{2,1,3,0:T(8,128)} %get-tuple-element.516, pred[512]{0:T(512)(128)(4,1)S(1)} %dynamic-slice_reduce_fusion.2), kind=kLoop, calls=%fused_computation.21.clone.1 | loop fusion | flops 29351936 | bytes 25231872 | tf_op jit(solution)/shard_map/while/body/eval_jaxpr/reduce_sum | solution.py:30
  323.7 11.8 %convert_reduce_fusion.4 = (f32[8,8,128]{2,1,0:T(8,128)S(1)}, bf16[8,8,128,512]{2,3,1,0:T(8,128)(2,1)}) fusion(f32[8,8,128]{2,1,0:T(8,128)S(1)} %select_maximum_fusion.4, f32[8,512,128,8]{2,1,3,0:T(8,128)} %get-tuple-element.516, pred[512]{0:T(512)(128)(4,1)S(1)} %dynamic-slice_reduce_fusion.2), kind=kLoop, calls=%fused_computation.21.clone.1 | loop fusion | flops 29351936 | bytes 25231872 | tf_op jit(solution)/shard_map/while/body/eval_jaxpr/reduce_sum | solution.py:30
  344.8 276.6 %all-gather.6.cloned.1.call-done = bf16[1,4096,2048]{1,2,0:T(8,128)(2,1)} async-done(((bf16[1,128,2048]{1,2,0:T(8,128)(2,1)}), bf16[1,4096,2048]{1,2,0:T(8,128)(2,1)}) %all-gather.6.cloned.1.call-update) | async-done | bytes 16777232 | tf_op jit(solution)/shard_map/all_gather | solution.py:117
  621.5 251.7 %conditional.1 = (f32[8,8,128]{2,1,0:T(8,128)S(1)}, f32[8,8,128]{2,1,0:T(8,128)S(1)}, f32[8,8,128,128]{3,2,1,0:T(8,128)}) conditional(s32[]{:T(128)} %convert_element_type.55, (s32[]{:T(128)}, s32[128,1]{0,1:T(1,128)S(1)}, s32[128,4096]{0,1:T(8,128)S(1)}, bf16[4096,2048]{0,1:T(8,128)(2,1)}, bf16[128,8,8,128]{0,3,2,1:T(8,128)(2,1)}) %tuple.113, () %tuple.43), branch_computations={%region_10.15_spmd, %region_15.16_spmd} | conditional | flops 2214109184 | bytes 141887360 | solution.py:120
  625.8 247.5 %while.35 = (s32[]{:T(128)}, f32[8,8,128]{2,1,0:T(8,128)S(1)}, f32[8,8,128]{2,1,0:T(8,128)S(1)}, f32[8,8,128,128]{3,2,1,0:T(8,128)}, pred[128,4096]{0,1:T(8,128)...) while((s32[]{:T(128)}, f32[8,8,128]{2,1,0:T(8,128)S(1)}, ...), condition=%wide.region_14.14_spmd.clone, body=%wide.region_11.13_spmd.clone.sunk | while | flops 2213584896 | bytes 135069936 | solution.py:46
  628.4 8.7 fusion.58
  637.2 8.2 convert_reduce_fusion.5
  647.8 8.6 fusion.60
  659.1 8.7 fusion.58
  678.5 8.9 fusion.60
  690.1 8.7 fusion.58
  698.8 8.2 convert_reduce_fusion.5
  709.4 8.9 fusion.60
  721.0 8.7 fusion.58
  740.4 8.9 fusion.60
  752.0 8.7 fusion.58
  760.8 8.2 convert_reduce_fusion.5
  771.4 8.9 fusion.60
  783.0 8.7 fusion.58
  791.7 8.2 convert_reduce_fusion.5
  802.4 8.9 fusion.60
  814.0 8.7 fusion.58
  822.7 8.2 convert_reduce_fusion.5
  833.3 8.9 fusion.60
  844.9 8.7 fusion.58
  864.3 8.9 fusion.60
  (159 shorter events, 180.1 us)
Async XLA Ops:
  6.5 1.5 copy-start
  6.5 17.7 %copy-start.3 = (bf16[1,128,8192]{2,1,0:T(8,128)(2,1)S(1)}, bf16[1,128,8192]{2,1,0:T(8,128)(2,1)}, u32[]{:S(2)}) copy-start(bf16[1,128,8192]{2,1,0:T(8,128)(2,1)} %param.11) | copy-start | bytes 6291460
  6.5 20.4 %copy-start.4 = (s32[256]{0:T(256)S(1)}, s32[256]{0:T(256)}, u32[]{:S(2)}) copy-start(s32[256]{0:T(256)} %param.15) | copy-start | bytes 3076
  6.5 204.6 %all-gather.4.cloned.1.call-start = ((), (), s32[]{:S(2)}) async-start(), calls=%async_computation.1 | async-start | bytes 8650752 | tf_op jit(solution)/shard_map/all_gather | solution.py:112
  7.5 20.8 %copy-start.5 = (u32[128]{0:T(128)S(1)}, u32[128]{0:T(128)}, u32[]{:S(2)}) copy-start(u32[128]{0:T(128)} %constant.199) | copy-start | bytes 1540
  21.3 600.1 %all-gather.6.cloned.1.call-start = ((), (), s32[]{:S(2)}) async-start(), calls=%async_computation.2 | async-start | bytes 17301504 | tf_op jit(solution)/shard_map/all_gather | solution.py:117
  637.2 10.6 %copy-start.2 = (f32[8,512,128,8]{2,1,3,0:T(8,128)S(1)}, f32[8,512,128,8]{2,1,3,0:T(8,128)}, u32[]{:S(2)}) copy-start(f32[8,512,128,8]{2,1,3,0:T(8,128)} %get-tuple-element.531) | copy-start | bytes 50331652 | tf_op jit(solution)/shard_map/cond/branch_0_fun/while
  667.8 10.6 %copy-start.2 = (f32[8,512,128,8]{2,1,3,0:T(8,128)S(1)}, f32[8,512,128,8]{2,1,3,0:T(8,128)}, u32[]{:S(2)}) copy-start(f32[8,512,128,8]{2,1,3,0:T(8,128)} %get-tuple-element.531) | copy-start | bytes 50331652 | tf_op jit(solution)/shard_map/cond/branch_0_fun/while
  698.8 10.6 %copy-start.2 = (f32[8,512,128,8]{2,1,3,0:T(8,128)S(1)}, f32[8,512,128,8]{2,1,3,0:T(8,128)}, u32[]{:S(2)}) copy-start(f32[8,512,128,8]{2,1,3,0:T(8,128)} %get-tuple-element.531) | copy-start | bytes 50331652 | tf_op jit(solution)/shard_map/cond/branch_0_fun/while
  729.8 10.6 %copy-start.2 = (f32[8,512,128,8]{2,1,3,0:T(8,128)S(1)}, f32[8,512,128,8]{2,1,3,0:T(8,128)}, u32[]{:S(2)}) copy-start(f32[8,512,128,8]{2,1,3,0:T(8,128)} %get-tuple-element.531) | copy-start | bytes 50331652 | tf_op jit(solution)/shard_map/cond/branch_0_fun/while
  760.8 10.6 %copy-start.2 = (f32[8,512,128,8]{2,1,3,0:T(8,128)S(1)}, f32[8,512,128,8]{2,1,3,0:T(8,128)}, u32[]{:S(2)}) copy-start(f32[8,512,128,8]{2,1,3,0:T(8,128)} %get-tuple-element.531) | copy-start | bytes 50331652 | tf_op jit(solution)/shard_map/cond/branch_0_fun/while
  791.7 10.6 %copy-start.2 = (f32[8,512,128,8]{2,1,3,0:T(8,128)S(1)}, f32[8,512,128,8]{2,1,3,0:T(8,128)}, u32[]{:S(2)}) copy-start(f32[8,512,128,8]{2,1,3,0:T(8,128)} %get-tuple-element.531) | copy-start | bytes 50331652 | tf_op jit(solution)/shard_map/cond/branch_0_fun/while
  822.7 10.6 %copy-start.2 = (f32[8,512,128,8]{2,1,3,0:T(8,128)S(1)}, f32[8,512,128,8]{2,1,3,0:T(8,128)}, u32[]{:S(2)}) copy-start(f32[8,512,128,8]{2,1,3,0:T(8,128)} %get-tuple-element.531) | copy-start | bytes 50331652 | tf_op jit(solution)/shard_map/cond/branch_0_fun/while
  853.7 10.6 %copy-start.2 = (f32[8,512,128,8]{2,1,3,0:T(8,128)S(1)}, f32[8,512,128,8]{2,1,3,0:T(8,128)}, u32[]{:S(2)}) copy-start(f32[8,512,128,8]{2,1,3,0:T(8,128)} %get-tuple-element.531) | copy-start | bytes 50331652 | tf_op jit(solution)/shard_map/cond/branch_0_fun/while
  873.2 11.2 %copy-start.1 = (bf16[2,16,2048]{2,1,0:T(8,128)(2,1)S(1)}, bf16[2,16,2048]{2,1,0:T(8,128)(2,1)}, u32[]{:S(2)}) copy-start(bf16[2,16,2048]{2,1,0:T(8,128)(2,1)} %param.13) | copy-start | bytes 393220
Sparse Core Ops, SparseCore 0:
  21.4 189.6 all-gather.3
  212.7 408.6 all-gather.5
where the time goes:
time: 899 us; the launch traced here: 891 us
  waiting for transfers between devices  383 us (43%)
  matrix products  203 us (23%)
  other arithmetic  122 us (14%)
  local copies, waits for them, and re-layouts  84.3 us (9%)
  blocking collectives  84.1 us (9%)
  between operations  14.2 us (2%)
    all_gather x1, waiting for transfers between devices, shards(): key_piece = lax.all_gather(stretch_kv[0], 'ctx', axis=0, tiled=True)  277 us
    reduce_sum x12, other arithmetic, update(): jnp.sum(weights, axis=-1, dtype=jnp.float32)  113 us
    all_gather x1, waiting for transfers between devices, shards(): lax.all_gather(tokens, 'ctx', axis=0, tiled=True)  107 us
    dot_general x12, matrix products, update(): jnp.einsum('kgtj,jkd->kgtd', weights, values, preferred_element_type=jnp....  102 us
    dot_general x12, matrix products, update(): jnp.einsum('tkgd,jkd->kgtj', query_heads, key_rows, preferred_element_typ...  101 us
    unnamed x1, blocking collectives  71.5 us
    slice x12, local copies, waits for them, and re-layouts, update(): values = key_block[:, half_width:].reshape(row_count, KV_HEADS, HEAD_DIM)  33.9 us
    while x36, local copies, waits for them, and re-layouts  30.8 us
  transfers between devices with their start and end apart: 2, of which 2 were waited for; matrix products, arithmetic and copies ran while one was open for 16% of the time, Pallas kernels for 0%

commit v1 on v0

v1 whole, which is shorter than its diff:
```python
import functools

import jax
import jax.numpy as jnp
from jax import lax
from jax.experimental import pallas as pl
from jax.experimental.pallas import tpu as pltpu
from jax.sharding import PartitionSpec as P

HEAD_DIM = 128
GROUP_HEADS = 8
KEY_HEADS = 2
ROWS = 128
N_REQ = 4
N_CTX = 32
PAGE = 16
CHUNK = 512
LOW = -1e30
SCALE = HEAD_DIM ** -0.5 * 1.4426950408889634
MESH = pl.DeviceIdType.MESH
Q_COLS = KEY_HEADS * GROUP_HEADS * HEAD_DIM
K_COLS = KEY_HEADS * HEAD_DIM
KV_COLS = 2 * K_COLS
V_AT = 1024
COMPUTE = True


def kernel(owner, fill, q_hbm, kv_hbm, pages, out_hbm, qbuf, kvbuf, pbuf, page_out, page_in, obuf, pbias,
           qs, acc, top, page_sems, gkv_sems, gq_sems, gp_sems, ckv_sems, cp_sems, o_sems, own_sems):
    req = lax.axis_index("req")
    ctx = lax.axis_index("ctx")
    x, y, z = ctx // 8, (ctx // 2) % 4, ctx % 2

    def place(cube, group):
        cube_x, cube_y, cube_z = cube % 2, (cube // 2) % 2, cube // 4
        group_x, group_y = group % 2, group // 2
        px = x + cube_x * (1 - 2 * (x % 2))
        py = y + cube_y * (1 - 2 * (y % 2))
        pz = z + cube_z * (1 - 2 * z)
        px = px + group_x * (3 - 2 * px)
        py = py + group_y * (3 - 2 * py)
        return px * 8 + py * 2 + pz

    def quarter(group):
        half_x, half_y = x // 2, y // 2
        half_x = half_x + (group % 2) * (1 - 2 * half_x)
        half_y = half_y + (group // 2) * (1 - 2 * half_y)
        return half_x * 2 + half_y

    def cols(start, size):
        return pl.ds(pl.multiple_of(start, 128), size)

    def remote(src, dst, sems, index, ctx_to, req_to=None):
        return pltpu.make_async_remote_copy(
            src_ref=src, dst_ref=dst, send_sem=sems.at[0, index], recv_sem=sems.at[1, index],
            device_id=(req if req_to is None else req_to, ctx_to), device_id_type=MESH)

    barrier = pltpu.get_barrier_semaphore()
    for step in range(1, N_REQ):
        pl.semaphore_signal(barrier, inc=1, device_id=((req + step) % N_REQ, ctx), device_id_type=MESH)
    for group in range(1, 4):
        pl.semaphore_signal(barrier, inc=1, device_id=(req, place(0, group)), device_id_type=MESH)
    for cube in (1, 2, 4):
        pl.semaphore_signal(barrier, inc=1, device_id=(req, place(cube, 0)), device_id_type=MESH)

    first_slot = (req * N_CTX + ctx) * 2
    for target in range(N_REQ):
        picked = jnp.where(owner[first_slot] == target, 0, 1)
        page_out[target] = pages[picked]
    page_in[pl.ds(req * PAGE, PAGE)] = page_out[req]
    mine = quarter(0)
    own_copies = [
        pltpu.make_async_copy(kv_hbm.at[0, :, cols(mine * K_COLS, K_COLS)], kvbuf.at[ctx, :, 0:K_COLS], own_sems.at[0]),
        pltpu.make_async_copy(
            kv_hbm.at[0, :, cols(V_AT + mine * K_COLS, K_COLS)], kvbuf.at[ctx, :, K_COLS:KV_COLS], own_sems.at[1]),
        pltpu.make_async_copy(q_hbm.at[0, :, cols(mine * Q_COLS, Q_COLS)], qbuf.at[0], own_sems.at[2]),
    ]
    for copy in own_copies:
        copy.start()
    pl.semaphore_wait(barrier, 9)

    started = []

    def start(copy):
        copy.start()
        started.append(copy)
        return copy

    page_copies = []
    for step in range(1, N_REQ):
        target = (req + step) % N_REQ
        page_copies.append(start(remote(
            page_out.at[target], page_in.at[pl.ds(req * PAGE, PAGE)], page_sems, step - 1, ctx, target)))
    kv_copies = []
    for group in range(1, 4):
        theirs = quarter(group)
        for part in range(2):
            kv_copies.append(start(remote(
                kv_hbm.at[0, :, cols(part * V_AT + theirs * K_COLS, K_COLS)],
                kvbuf.at[ctx, :, part * K_COLS:(part + 1) * K_COLS],
                gkv_sems, group * 2 + part, place(0, group))))
    q_copies = []
    for group in range(1, 4):
        q_copies.append(start(remote(
            q_hbm.at[0, :, cols(quarter(group) * Q_COLS, Q_COLS)], qbuf.at[group], gq_sems, group, place(0, group))))

    for copy in page_copies:
        copy.wait_recv()
    group_pages = []
    for group in range(1, 4):
        theirs = quarter(group)
        for part in range(2):
            group_pages.append(start(remote(
                page_in.at[:, cols(part * V_AT + theirs * K_COLS, K_COLS)],
                pbuf.at[0, group, :, part * K_COLS:(part + 1) * K_COLS],
                gp_sems, group * 2 + part, place(0, group))))
    pbuf[0, 0, :, 0:K_COLS] = page_in[:, cols(mine * K_COLS, K_COLS)]
    pbuf[0, 0, :, K_COLS:KV_COLS] = page_in[:, cols(V_AT + mine * K_COLS, K_COLS)]

    arriving = {}

    def send_prefix(held, bit):
        arriving["p", held ^ bit] = [start(remote(
            pbuf.at[held], pbuf.at[held ^ bit], cp_sems, held ^ bit, place(bit, 0)))]

    def send_blocks(name, members, held, bit):
        arriving[name, held ^ bit] = [
            start(remote(kvbuf.at[place(held, group)], kvbuf.at[place(held, group)], ckv_sems,
                         (held ^ bit) * 4 + group, place(bit, 0)))
            for group in members]

    orders = {"a": (2, 4, 1), "b": (4, 1, 2), "p": (1, 2, 4)}
    held = {"a": [0], "b": [0], "p": [0]}
    for copy in own_copies[:2]:
        copy.wait()
    for copy in kv_copies:
        copy.wait_recv()
    for step in range(3):
        for name in ("a", "b", "p"):
            if step == 0 and name == "p":
                for copy in group_pages:
                    copy.wait_recv()
            if step > 0:
                for index in held[name]:
                    for copy in arriving.pop((name, index), []):
                        copy.wait_recv()
            bit = orders[name][step]
            for index in held[name]:
                if name == "p":
                    send_prefix(index, bit)
                else:
                    send_blocks(name, (0, 1) if name == "a" else (2, 3), index, bit)
            held[name] = held[name] + [index ^ bit for index in held[name]]

    lane = lax.broadcasted_iota(jnp.int32, (1, 8 * 4 * N_REQ * PAGE), 1)

    def count_page(index, counts):
        source = place(index // 16, (index // 4) % 4)
        slot = ((index % 4) * N_CTX + source) * 2
        written = jnp.where(owner[slot] == req, fill[slot], jnp.where(owner[slot + 1] == req, fill[slot + 1], 0))
        return jnp.where(lane // PAGE == index, written, counts)

    counts = lax.fori_loop(0, 8 * 4 * N_REQ, count_page, jnp.zeros_like(lane))
    pbias[...] = jnp.where(lane % PAGE < counts, 0.0, LOW)

    own_copies[2].wait()
    for copy in q_copies:
        copy.wait_recv()
    for copies in arriving.values():
        for copy in copies:
            copy.wait_recv()

    ones = jnp.ones((CHUNK, HEAD_DIM), jnp.bfloat16)

    def product(head, keys):
        return lax.dot_general(qs[head], keys, (((1,), (1,)), ((), ())), preferred_element_type=jnp.float32)

    def absorb(head, scores, values):
        old = top[head]
        new = jnp.maximum(old, jnp.max(scores, axis=-1, keepdims=True))
        factor = jnp.exp2((old - new) * SCALE)
        weights = jnp.exp2((scores - jnp.tile(new, (1, CHUNK // HEAD_DIM))) * SCALE).astype(jnp.bfloat16)
        summed = jnp.dot(weights, jnp.concatenate([values, ones], axis=1), preferred_element_type=jnp.float32)
        acc[head] = acc[head] * jnp.tile(factor, (1, 2)) + summed
        top[head] = new

    def out_copy(member, slot):
        return remote(obuf.at[member], out_hbm.at[0, :, cols(mine * Q_COLS, Q_COLS)], o_sems, slot, place(0, member))

    def attend(turn, _):
        member = (turn + 1) % 4
        position = place(0, member)
        for head in range(KEY_HEADS):
            for g in range(GROUP_HEADS):
                at = (head * GROUP_HEADS + g) * HEAD_DIM
                qs[head, g * ROWS:(g + 1) * ROWS, :] = qbuf[member, :, at:at + HEAD_DIM]
            acc[head] = jnp.zeros((GROUP_HEADS * ROWS, 2 * HEAD_DIM), jnp.float32)
            top[head] = jnp.full((GROUP_HEADS * ROWS, HEAD_DIM), LOW, jnp.float32)

        def prefix_step(step, _):
            block = pbuf[pl.ds(step * 2, 2)].reshape(CHUNK, KV_COLS)
            bias = pbias[:, pl.ds(pl.multiple_of(step * CHUNK, CHUNK), CHUNK)]
            for head in range(KEY_HEADS):
                at = head * HEAD_DIM
                absorb(head, product(head, block[:, at:at + HEAD_DIM]) + bias,
                       block[:, K_COLS + at:K_COLS + at + HEAD_DIM])
            return 0

        def stretch(step, masked):
            block = kvbuf[pl.ds(step * 4, 4)].reshape(CHUNK, KV_COLS)
            for head in range(KEY_HEADS):
                at = head * HEAD_DIM
                scores = product(head, block[:, at:at + HEAD_DIM])
                if masked:
                    ahead = (lax.broadcasted_iota(jnp.int32, scores.shape, 1)
                             - lax.broadcasted_iota(jnp.int32, scores.shape, 0) % ROWS)
                    scores = jnp.where(ahead <= position * ROWS - step * CHUNK, scores, LOW)
                absorb(head, scores, block[:, K_COLS + at:K_COLS + at + HEAD_DIM])
            return 0

        if COMPUTE:
            lax.fori_loop(0, 4, prefix_step, 0)
            lax.fori_loop(0, position // 4, lambda step, _: stretch(step, False), 0)
            stretch(position // 4, True)
        for head in range(KEY_HEADS):
            result = (acc[head, :, :HEAD_DIM] / acc[head, :, HEAD_DIM:]).astype(jnp.bfloat16)
            for g in range(GROUP_HEADS):
                at = (head * GROUP_HEADS + g) * HEAD_DIM
                obuf[member, :, at:at + HEAD_DIM] = result[g * ROWS:(g + 1) * ROWS]

        @pl.when(turn < 3)
        def _():
            out_copy(member, member).start()

        return 0

    lax.fori_loop(0, 4, attend, 0)
    last = pltpu.make_async_copy(obuf.at[0], out_hbm.at[0, :, cols(mine * Q_COLS, Q_COLS)], own_sems.at[3])
    last.start()
    for member in range(1, 4):
        out_copy(member, member).wait_recv()
    for copy in started:
        copy.wait_send()
    for member in range(1, 4):
        out_copy(member, member).wait_send()
    last.wait()


def shards(queries, stretch_kv, page_pool, slot_owner, slot_fill):
    vmem = pltpu.VMEM
    dma = pltpu.SemaphoreType.DMA
    wide = GROUP_HEADS * ROWS
    smem_spec = pl.BlockSpec(memory_space=pltpu.SMEM)
    any_spec = pl.BlockSpec(memory_space=pl.ANY)
    return pl.pallas_call(
        kernel,
        out_shape=jax.ShapeDtypeStruct(queries.shape, jnp.bfloat16),
        in_specs=[smem_spec, smem_spec, any_spec, any_spec, pl.BlockSpec(memory_space=vmem)],
        out_specs=any_spec,
        scratch_shapes=[
            vmem((4, ROWS, Q_COLS), jnp.bfloat16),
            vmem((N_CTX, ROWS, KV_COLS), jnp.bfloat16),
            vmem((8, 4, N_REQ * PAGE, KV_COLS), jnp.bfloat16),
            vmem((N_REQ, PAGE, 2048), jnp.bfloat16),
            vmem((N_REQ * PAGE, 2048), jnp.bfloat16),
            vmem((4, ROWS, Q_COLS), jnp.bfloat16),
            vmem((1, 8 * 4 * N_REQ * PAGE), jnp.float32),
            vmem((KEY_HEADS, wide, HEAD_DIM), jnp.bfloat16),
            vmem((KEY_HEADS, wide, 2 * HEAD_DIM), jnp.float32),
            vmem((KEY_HEADS, wide, HEAD_DIM), jnp.float32),
            dma((2, 3)),
            dma((2, 8)),
            dma((2, 4)),
            dma((2, 8)),
            dma((2, 32)),
            dma((2, 8)),
            dma((2, 4)),
            dma((4,)),
        ],
        compiler_params=pltpu.CompilerParams(
            collective_id=0, has_side_effects=True, vmem_limit_bytes=56 * 2 ** 20),
        cost_estimate=pl.CostEstimate(flops=18 * 10 ** 9, bytes_accessed=6 * 10 ** 6, transcendentals=40 * 10 ** 6),
    )(slot_owner, slot_fill, queries, stretch_kv, page_pool)


def solution(mesh):
    placed = (P("req", "ctx", None), P("req", "ctx", None), P(("req", "ctx"), None, None), P(), P())
    return jax.shard_map(
        shards, mesh=mesh, in_specs=placed, out_specs=P("req", "ctx", None), check_vma=False
    )
```

time: 899 us -> 152 us (0.17)
  waiting for transfers between devices: 383 us -> 0 us
  matrix products: 203 us -> 0 us
  Pallas kernels: 0 us -> 148 us
  other arithmetic: 122 us -> 0 us
  blocking collectives: 84.1 us -> 0 us
  local copies, waits for them, and re-layouts: 84.3 us -> 3.1 us
  between operations: 14.2 us -> 0.01 us
    all_gather x2 -> x0, waiting for transfers between devices: 383 us -> none  [the longest x1 277 us: shards(): key_piece = lax.all_gather(stretch_kv[0], 'ctx', axis=0, tiled=True)]
    dot_general x24 -> x0, matrix products: 203 us -> none  [the longest x12 102 us: update(): jnp.einsum('kgtj,jkd->kgtd', weights, values, preferred_element_type=jnp....]
    pallas_call x0 -> x1, Pallas kernels: none -> 148 us  [shards(): pl.pallas_call(kernel, out_shape=jax.ShapeDtypeStruct(queries.shape, jnp....]
    reduce_sum x14 -> x0, other arithmetic: 113 us -> none  [the longest x12 113 us: update(): jnp.sum(weights, axis=-1, dtype=jnp.float32)]
    unnamed x1 -> x0, blocking collectives: 71.5 us -> none
    slice x12 -> x0, local copies, waits for them, and re-layouts: 33.9 us -> none  [update(): values = key_block[:, half_width:].reshape(row_count, KV_HEADS, HEAD_DIM)]
    while x36 -> x0, local copies, waits for them, and re-layouts: 30.8 us -> none
    all_to_all x1 -> x0, blocking collectives: 12.6 us -> none  [shards(): lax.all_to_all(per_request, 'req', split_axis=0, concat_axis=0, tiled=True)]
  transfers between devices with their start and end apart: 2 -> 0, of which waited for: 2 -> 0; matrix products, arithmetic and copies ran while one was open for 16% -> 0% of each run, Pallas kernels for 0% -> 0%
where the time goes in v1:
time: 152 us; the launch traced here: 151 us
  Pallas kernels  148 us (97%)
  local copies, waits for them, and re-layouts  3.1 us (2%)
    pallas_call x1, Pallas kernels, shards(): pl.pallas_call(kernel, out_shape=jax.ShapeDtypeStruct(queries.shape, jnp....  148 us
    unnamed x1, local copies, waits for them, and re-layouts  3.1 us

profile of v1, /device:TPU:2, one launch (start us, length us, event | category | flops | bytes accessed | tf_op | source)
XLA Modules:
  0.0 151.5 jit_solution(5070224471767643384)
XLA Ops:
  0.0 148.3 %shard_map.55 = bf16[1,128,8192]{2,1,0:T(8,128)(2,1)} custom-call(s32[256]{0:T(256)} %owner.1, s32[256]{0:T(256)} %fill.1, bf16[1,128,8192]{2,1,0:T(8,128)(2,1)} %q_hbm.1, bf16[1,128,2048]{2,1,0:T(8,128)(2,1)} %kv_hbm.1, bf16[2,16,2048]{2,1,0:T(8,128)(2,1)} %pages.1), custom_call_target="tpu_custom_call" | custom-call | flops 17999998976 | bytes 6000000 | tf_op jit(solution)/shard_map/pallas_call | solution.py:255
  148.4 3.1 %copy.7 = bf16[1,128,8192]{2,1,0:T(8,128)(2,1)} copy(bf16[1,128,8192]{2,1,0:T(8,128)(2,1)} %shard_map.55) | data formatting | bytes 4194304

commit v2 on v1

v2 whole, which is shorter than its diff:
```python
import functools

import jax
import jax.numpy as jnp
from jax import lax
from jax.experimental import pallas as pl
from jax.experimental.pallas import tpu as pltpu
from jax.sharding import PartitionSpec as P

HEAD_DIM = 128
GROUP_HEADS = 8
ROWS = 128
MEMBERS = 8
SQUARE = 4
N_REQ = 4
N_CTX = 32
PAGE = 16
V_AT = 1024
CHUNK = 512
ROOM = 768
PREFIX_ROWS = 2048
WIDE = GROUP_HEADS * ROWS
Q_COLS = GROUP_HEADS * HEAD_DIM
LOW = -1e30
SCALE = HEAD_DIM ** -0.5 * 1.4426950408889634
MESH = pl.DeviceIdType.MESH
COMPUTE = True


def kernel(room, owner, fill, q_hbm, kv_hbm, pages, out_hbm, q_own, qbuf, near_kv, far_kv, pbuf, packed, page_out, page_in, obuf,
           pbias, acc, top, held, held_prefix, page_sems, gkv_sems, gq_sems, gp_sems, sq_sems, sp_sems, o_sems, own_sems):
    req = lax.axis_index("req")
    ctx = lax.axis_index("ctx")
    x, y, z = ctx // 8, (ctx // 2) % 4, ctx % 2

    def spot(square, group):
        px = x + (square % 2) * (1 - 2 * (x % 2))
        py = y + (square // 2) * (1 - 2 * (y % 2))
        px = px + (group // 4) * (3 - 2 * px)
        py = py + ((group // 2) % 2) * (3 - 2 * py)
        return px, py, z + (group % 2) * (1 - 2 * z)

    def place(square, group):
        px, py, pz = spot(square, group)
        return px * 8 + py * 2 + pz

    def head_of(group):
        px, py, pz = spot(0, group)
        return (px // 2) * 4 + (py // 2) * 2 + pz

    def cols(start, size):
        return pl.ds(pl.multiple_of(start, 128), size)

    def remote(src, dst, sems, index, ctx_to, req_to=None):
        return pltpu.make_async_remote_copy(
            src_ref=src, dst_ref=dst, send_sem=sems.at[0, index], recv_sem=sems.at[1, index],
            device_id=(req if req_to is None else req_to, ctx_to), device_id_type=MESH)

    barrier = pltpu.get_barrier_semaphore()
    for step in range(1, N_REQ):
        pl.semaphore_signal(barrier, inc=1, device_id=((req + step) % N_REQ, ctx), device_id_type=MESH)
    for group in range(1, MEMBERS):
        pl.semaphore_signal(barrier, inc=1, device_id=(req, place(0, group)), device_id_type=MESH)
    for square in (1, 2):
        pl.semaphore_signal(barrier, inc=1, device_id=(req, place(square, 0)), device_id_type=MESH)

    first_slot = (req * N_CTX + ctx) * 2
    for target in range(N_REQ):
        picked = jnp.where(owner[first_slot] == target, 0, 1)
        page_out[target] = pages[picked]
    page_in[pl.ds(req * PAGE, PAGE)] = page_out[req]
    mine = head_of(0)

    def kv_piece(group, part):
        head = head_of(group)
        return (kv_hbm.at[0, :, cols(part * V_AT + head * HEAD_DIM, HEAD_DIM)],
                near_kv.at[0, group, :, part * HEAD_DIM:(part + 1) * HEAD_DIM])

    def q_copy(group):
        return remote(q_hbm.at[0, :, cols(head_of(group) * Q_COLS, Q_COLS)], qbuf.at[group], gq_sems, group,
                      place(0, group))

    own_kv = [pltpu.make_async_copy(*kv_piece(0, part), own_sems.at[part]) for part in range(2)]
    own_q = pltpu.make_async_copy(q_hbm.at[0, :, cols(mine * Q_COLS, Q_COLS)], q_own, own_sems.at[2])
    for copy in own_kv:
        copy.start()
    own_q.start()
    pl.semaphore_wait(barrier, N_REQ - 1 + MEMBERS - 1 + 2)

    started = []

    def start(copy):
        copy.start()
        started.append(copy)
        return copy

    page_copies = []
    for step in range(1, N_REQ):
        target = (req + step) % N_REQ
        page_copies.append(start(remote(
            page_out.at[target], page_in.at[pl.ds(req * PAGE, PAGE)], page_sems, step - 1, ctx, target)))
    near = (1, 2, 4, 3, 5, 6, 7)
    kv_copies = {0: own_kv}
    for group in near:
        kv_copies[group] = [
            start(remote(*kv_piece(group, part), gkv_sems, group * 2 + part, place(0, group)))
            for part in range(2)]

    for copy in page_copies:
        copy.wait_recv()
    group_pages = []
    for group in near:
        theirs = head_of(group)
        for part in range(2):
            group_pages.append(start(remote(
                page_in.at[:, cols(part * V_AT + theirs * HEAD_DIM, HEAD_DIM)],
                pbuf.at[0, group, :, part * HEAD_DIM:(part + 1) * HEAD_DIM],
                gp_sems, group * 2 + part, place(0, group))))
    for part in range(2):
        pbuf[0, 0, :, part * HEAD_DIM:(part + 1) * HEAD_DIM] = page_in[:, cols(part * V_AT + mine * HEAD_DIM, HEAD_DIM)]

    def pass_block(slot, group, bit):
        source = near_kv.at[slot // 2, group]
        target = (far_kv if bit == 1 else near_kv).at[(slot + bit) // 2, group]
        return start(remote(source, target, sq_sems, (slot + bit) * MEMBERS + group, place(bit, 0)))

    def pass_prefix(slot, bit):
        return start(remote(pbuf.at[slot], pbuf.at[slot + bit], sp_sems, slot + bit, place(bit, 0)))

    blocks = {1: [], 2: [], 3: []}
    for group in (0,) + near:
        for copy in kv_copies[group]:
            copy.wait() if group == 0 else copy.wait_recv()
        blocks[2].append(pass_block(0, group, 2))
        blocks[1].append(pass_block(0, group, 1))
    for copy in group_pages:
        copy.wait_recv()
    prefixes = {1: pass_prefix(0, 1), 2: pass_prefix(0, 2)}
    for group in near:
        start(q_copy(group))

    def product(member, keys, queries_of=None):
        queries_of = qbuf.at[member] if queries_of is None else queries_of
        queries = jnp.concatenate(
            [queries_of[:, g * HEAD_DIM:(g + 1) * HEAD_DIM] for g in range(GROUP_HEADS)], axis=0)
        return lax.dot_general(queries, keys, (((1,), (1,)), ((), ())), preferred_element_type=jnp.float32)

    def weigh(scores, new, values):
        size = scores.shape[1]
        weights = jnp.exp2((scores - jnp.tile(new, (1, size // HEAD_DIM))) * SCALE).astype(jnp.bfloat16)
        ones = jnp.ones((size, HEAD_DIM), jnp.bfloat16)
        return jnp.dot(weights, jnp.concatenate([values, ones], axis=1), preferred_element_type=jnp.float32)

    def begin(member, scores, values):
        new = jnp.broadcast_to(jnp.max(scores, axis=-1, keepdims=True), (WIDE, HEAD_DIM))
        acc[member] = weigh(scores, new, values)
        top[member] = new

    def absorb(member, scores, values):
        old = top[member]
        new = jnp.maximum(old, jnp.max(scores, axis=-1, keepdims=True))
        factor = jnp.exp2((old - new) * SCALE)
        acc[member] = acc[member] * jnp.tile(factor, (1, 2)) + weigh(scores, new, values)
        top[member] = new

    def keys_of(buffer, which, half):
        return buffer[which, pl.ds(half * 4, 4), :, 0:HEAD_DIM].reshape(CHUNK, HEAD_DIM)

    def values_of(buffer, which, half):
        return buffer[which, pl.ds(half * 4, 4), :, HEAD_DIM:2 * HEAD_DIM].reshape(CHUNK, HEAD_DIM)

    def mask(scores, square, member):
        _, py, pz = spot(0, member)
        _, key_y, _ = spot(square, 0)
        lane = lax.broadcasted_iota(jnp.int32, (1, CHUNK), 1)
        from_y, from_z = lane // (2 * ROWS), (lane // ROWS) % 2
        at_y = key_y + from_y * (3 - 2 * key_y)
        at_z = z + from_z * (1 - 2 * z)
        token = (at_y * 2 + at_z - (py * 2 + pz)) * ROWS + lane % ROWS
        row = lax.broadcasted_iota(jnp.int32, (WIDE, 1), 0) % ROWS
        return jnp.where(token <= row, scores, LOW)

    def near_keys(member, queries_of=None):
        px, py, _ = spot(0, member)
        half = member // 4
        held[0] = product(member, keys_of(near_kv, 0, half), queries_of)

        @pl.when(px >= 2)
        def _():
            held[1] = product(member, keys_of(near_kv, 0, 1 - half), queries_of)
            begin(member, mask(held[0], 0, member), values_of(near_kv, 0, half))
            held[0] = product(member, keys_of(near_kv, 1, half), queries_of)
            absorb(member, held[1], values_of(near_kv, 0, 1 - half))
            held[1] = product(member, keys_of(near_kv, 1, 1 - half), queries_of)
            absorb(member, mask(held[0], 2, member), values_of(near_kv, 1, half))
            absorb(member, held[1], values_of(near_kv, 1, 1 - half))

        @pl.when((px < 2) & (py > 0))
        def _():
            held[1] = product(member, keys_of(near_kv, 1, half), queries_of)
            begin(member, mask(held[0], 0, member), values_of(near_kv, 0, half))
            absorb(member, mask(held[1], 2, member), values_of(near_kv, 1, half))

        @pl.when((px < 2) & (py == 0))
        def _():
            begin(member, mask(held[0], 0, member), values_of(near_kv, 0, half))

    def x_half():
        return spot(1, 0)[0] // 3

    row = (lax.broadcasted_iota(jnp.int32, (PAGE, HEAD_DIM), 0) * HEAD_DIM
           + lax.broadcasted_iota(jnp.int32, (PAGE, HEAD_DIM), 1))

    def count_page(index, carry):
        places, before = carry
        source = place(index // (MEMBERS * N_REQ), (index // N_REQ) % MEMBERS)
        slot = ((index % N_REQ) * N_CTX + source) * 2
        written = jnp.where(owner[slot] == req, fill[slot], jnp.where(owner[slot + 1] == req, fill[slot + 1], 0))
        token = row - index * PAGE
        inside = (token >= 0) & (token < written)
        return jnp.where(inside, token + before, places), before + written

    places, total = lax.fori_loop(0, PREFIX_ROWS // PAGE, count_page, (jnp.full_like(row, -1), jnp.int32(0)))
    pbias[...] = jnp.where(lax.broadcasted_iota(jnp.int32, (1, room), 1) < total, 0.0, LOW)

    for group, copy in zip((0,) + near, blocks[2], strict=True):
        copy.wait_recv()
        blocks[3].append(pass_block(2, group, 1))
    prefixes[1].wait_recv()
    prefixes[3] = pass_prefix(1, 2)
    own_q.wait()
    if COMPUTE:
        near_keys(0, q_own)
    qbuf[0] = q_own[...]
    for group in near:
        q_copy(group).wait_recv()
    if COMPUTE:
        lax.fori_loop(1, MEMBERS, lambda member, _: (near_keys(member), 0)[1], 0)

    prefixes[2].wait_recv()
    prefixes[3].wait_recv()
    if COMPUTE:
        for at in range(0, room, 256):
            wanted = lax.broadcasted_iota(jnp.int32, (256, HEAD_DIM), 0) + at
            chosen = jnp.concatenate(
                [jnp.where(wanted == places[k:k + 1], 1.0, 0.0).astype(jnp.bfloat16) for k in range(PAGE)], axis=1)
            packed[at:at + 256] = jnp.dot(
                chosen, pbuf[...].reshape(PREFIX_ROWS, 2 * HEAD_DIM), preferred_element_type=jnp.float32
            ).astype(jnp.bfloat16)

    for copy in blocks[1] + blocks[3]:
        copy.wait_recv()

    def out_copy(member):
        return remote(obuf.at[member], out_hbm.at[0, :, cols(mine * Q_COLS, Q_COLS)], o_sems, member, place(0, member))

    piece = ROOM if room == ROOM else CHUNK

    def prefix_scores(member, at):
        return product(member, packed[at:at + piece, 0:HEAD_DIM]) + pbias[:, at:at + piece]

    def absorb_prefix(member, at, scores):
        absorb(member, scores, packed[at:at + piece, HEAD_DIM:2 * HEAD_DIM])

    def other_keys(turn, _):
        member = MEMBERS - 1 - turn
        px, _, _ = spot(0, member)
        if COMPUTE:
            held_prefix[:, :piece] = prefix_scores(member, 0)

            @pl.when(px == 3)
            def _():
                held[0] = product(member, keys_of(far_kv, 0, 0))
                absorb_prefix(member, 0, held_prefix[:, :piece])
                held[1] = product(member, keys_of(far_kv, 0, 1))
                absorb(member, held[0], values_of(far_kv, 0, 0))
                held[0] = product(member, keys_of(far_kv, 1, 0))
                absorb(member, held[1], values_of(far_kv, 0, 1))
                held[1] = product(member, keys_of(far_kv, 1, 1))
                absorb(member, held[0], values_of(far_kv, 1, 0))
                absorb(member, held[1], values_of(far_kv, 1, 1))

            @pl.when((px == 1) | (px == 2))
            def _():
                half = x_half()
                held[0] = product(member, keys_of(far_kv, 0, half))
                absorb_prefix(member, 0, held_prefix[:, :piece])
                held[1] = product(member, keys_of(far_kv, 1, half))
                absorb(member, held[0], values_of(far_kv, 0, half))
                absorb(member, held[1], values_of(far_kv, 1, half))

            @pl.when(px == 0)
            def _():
                absorb_prefix(member, 0, held_prefix[:, :piece])

            for at in range(piece, room, piece):
                absorb_prefix(member, at, prefix_scores(member, at))
        result = (acc[member, :, :HEAD_DIM] / acc[member, :, HEAD_DIM:]).astype(jnp.bfloat16)
        for g in range(GROUP_HEADS):
            obuf[member, :, g * HEAD_DIM:(g + 1) * HEAD_DIM] = result[g * ROWS:(g + 1) * ROWS]

        @pl.when(member > 0)
        def _():
            out_copy(member).start()

        return 0

    lax.fori_loop(0, MEMBERS, other_keys, 0)
    last_copy = pltpu.make_async_copy(obuf.at[0], out_hbm.at[0, :, cols(mine * Q_COLS, Q_COLS)], own_sems.at[3])
    last_copy.start()
    for copy in started:
        copy.wait_send()
    for member in range(1, MEMBERS):
        out_copy(member).wait_recv()
        out_copy(member).wait_send()
    last_copy.wait()


def attend(room, queries, stretch_kv, page_pool, slot_owner, slot_fill):
    vmem = pltpu.VMEM
    dma = pltpu.SemaphoreType.DMA
    smem_spec = pl.BlockSpec(memory_space=pltpu.SMEM)
    any_spec = pl.BlockSpec(memory_space=pl.ANY)
    return pl.pallas_call(
        functools.partial(kernel, room),
        out_shape=jax.ShapeDtypeStruct(queries.shape, jnp.bfloat16),
        in_specs=[smem_spec, smem_spec, any_spec, any_spec, pl.BlockSpec(memory_space=vmem)],
        out_specs=any_spec,
        scratch_shapes=[
            vmem((ROWS, Q_COLS), jnp.bfloat16),
            vmem((MEMBERS, ROWS, Q_COLS), jnp.bfloat16),
            vmem((SQUARE // 2, MEMBERS, ROWS, 2 * HEAD_DIM), jnp.bfloat16),
            vmem((SQUARE // 2, MEMBERS, ROWS, 2 * HEAD_DIM), jnp.bfloat16),
            vmem((SQUARE, MEMBERS, N_REQ * PAGE, 2 * HEAD_DIM), jnp.bfloat16),
            vmem((room, 2 * HEAD_DIM), jnp.bfloat16),
            vmem((N_REQ, PAGE, 2048), jnp.bfloat16),
            vmem((N_REQ * PAGE, 2048), jnp.bfloat16),
            vmem((MEMBERS, ROWS, Q_COLS), jnp.bfloat16),
            vmem((1, room), jnp.float32),
            vmem((MEMBERS, WIDE, 2 * HEAD_DIM), jnp.float32),
            vmem((MEMBERS, WIDE, HEAD_DIM), jnp.float32),
            vmem((2, WIDE, CHUNK), jnp.float32),
            vmem((WIDE, ROOM), jnp.float32),
            dma((2, N_REQ - 1)),
            dma((2, 2 * MEMBERS)),
            dma((2, MEMBERS)),
            dma((2, 2 * MEMBERS)),
            dma((2, SQUARE * MEMBERS)),
            dma((2, SQUARE)),
            dma((2, MEMBERS)),
            dma((4,)),
        ],
        compiler_params=pltpu.CompilerParams(
            collective_id=0 if room == ROOM else 1, has_side_effects=True, vmem_limit_bytes=58 * 2 ** 20),
        cost_estimate=pl.CostEstimate(flops=12 * 10 ** 9, bytes_accessed=6 * 10 ** 6, transcendentals=25 * 10 ** 6),
    )(slot_owner, slot_fill, queries, stretch_kv, page_pool)


def shards(queries, stretch_kv, page_pool, slot_owner, slot_fill):
    requests = jnp.arange(N_REQ, dtype=jnp.int32)[:, None]
    tokens = jnp.sum(jnp.where(slot_owner[None] == requests, slot_fill[None], 0), axis=1)
    return lax.cond(
        jnp.max(tokens) <= ROOM, functools.partial(attend, ROOM), functools.partial(attend, PREFIX_ROWS),
        queries, stretch_kv, page_pool, slot_owner, slot_fill)


def solution(mesh):
    placed = (P("req", "ctx", None), P("req", "ctx", None), P(("req", "ctx"), None, None), P(), P())
    return jax.shard_map(
        shards, mesh=mesh, in_specs=placed, out_specs=P("req", "ctx", None), check_vma=False
    )
```

time: 152 us -> 111 us (0.73)
  the two profiles are of different devices: /device:TPU:2 before, /device:TPU:6 now
where the time goes in v2:
time: 111 us
  Pallas kernels  107 us (96%)
  other arithmetic  1.45 us (1%)
  local copies, waits for them, and re-layouts  1.32 us (1%)
    pallas_call x1, Pallas kernels, attend(): pl.pallas_call(functools.partial(kernel, room), out_shape=jax.ShapeDtypeS...  107 us

profile of v2, /device:TPU:6, one launch (start us, length us, event | category | flops | bytes accessed | tf_op | source)
XLA Modules:
  0.0 111.1 jit_solution(899798137516341479)
XLA Ops:
  0.0 0.8 select_reduce_fusion
  0.8 0.6 reduce_max.9
  2.1 107.7 %conditional.1 = (bf16[1,128,8192]{2,1,0:T(8,128)(2,1)S(1)}) conditional(s32[]{:T(128)} %convert_element_type.3, (s32[256]{0:T(256)}, s32[256]{0:T(256)}, bf16[1,128,8192]{2,1,0:T(8,128)(2,1)}, bf16[1,128,2048]{2,1,0:T(8,128)(2,1)}, bf16[2,16,2048]{2,1,0:T(8,128)(2,1)}) %tuple.11, (s32[256]{0:T(256)}, s32[256]{0:T(256)}, ...), branch_computations={%region_2.3_spmd, %region_3.4_spmd} | conditional | flops 12000000000 | bytes 6000008 | solution.py:362
  2.3 107.1 %branch_1_fun.1 = bf16[1,128,8192]{2,1,0:T(8,128)(2,1)S(1)} custom-call(s32[256]{0:T(256)} %get-tuple-element.33.owner, s32[256]{0:T(256)} %get-tuple-element.34.fill, bf16[1,128,8192]{2,1,0:T(8,128)(2,1)} %get-tuple-element.46.q_hbm, bf16[1,128,2048]{2,1,0:T(8,128)(2,1)} %get-tuple-element.48.kv_hbm, bf16[2,16,2048]{2,1,0:T(8,128)(2,1)} %get-tuple-element.50.pages), custom_call_target="tpu_custom_call" | custom-call | flops 12000000000 | bytes 6000000 | tf_op jit(solution)/shard_map/cond/branch_1_fun/pallas_call | solution.py:324
  109.8 1.3 %copy.17 = bf16[1,128,8192]{2,1,0:T(8,128)(2,1)} copy(bf16[1,128,8192]{2,1,0:T(8,128)(2,1)S(1)} %get-tuple-element.38) | data formatting | bytes 4194304

commit v3 on v2

--- a/solution.py
+++ b/solution.py
@@ -27,7 +27,7 @@
 COMPUTE = True
 
 
-def kernel(room, owner, fill, q_hbm, kv_hbm, pages, out_hbm, q_own, qbuf, near_kv, far_kv, pbuf, packed, page_out, page_in, obuf,
+def kernel(room, owner, fill, q_hbm, kv_hbm, pages, out_hbm, q_first, q_second, qbuf, near_kv, far_kv, pbuf, packed, page_out, page_in, obuf,
            pbias, acc, top, held, held_prefix, page_sems, gkv_sems, gq_sems, gp_sems, sq_sems, sp_sems, o_sems, own_sems):
     req = lax.axis_index("req")
     ctx = lax.axis_index("ctx")
@@ -71,17 +71,19 @@
     page_in[pl.ds(req * PAGE, PAGE)] = page_out[req]
     mine = head_of(0)
 
+    near = (1, 2, 4, 3, 5, 6, 7)
+
     def kv_piece(group, part):
         head = head_of(group)
         return (kv_hbm.at[0, :, cols(part * V_AT + head * HEAD_DIM, HEAD_DIM)],
                 near_kv.at[0, group, :, part * HEAD_DIM:(part + 1) * HEAD_DIM])
 
     def q_copy(group):
-        return remote(q_hbm.at[0, :, cols(head_of(group) * Q_COLS, Q_COLS)], qbuf.at[group], gq_sems, group,
-                      place(0, group))
+        landing = q_first.at[near.index(group) + 1] if group in near[:3] else q_second.at[near.index(group) - 3]
+        return remote(q_hbm.at[0, :, cols(head_of(group) * Q_COLS, Q_COLS)], landing, gq_sems, group, place(0, group))
 
     own_kv = [pltpu.make_async_copy(*kv_piece(0, part), own_sems.at[part]) for part in range(2)]
-    own_q = pltpu.make_async_copy(q_hbm.at[0, :, cols(mine * Q_COLS, Q_COLS)], q_own, own_sems.at[2])
+    own_q = pltpu.make_async_copy(q_hbm.at[0, :, cols(mine * Q_COLS, Q_COLS)], q_first.at[0], own_sems.at[2])
     for copy in own_kv:
         copy.start()
     own_q.start()
@@ -99,12 +101,13 @@
         target = (req + step) % N_REQ
         page_copies.append(start(remote(
             page_out.at[target], page_in.at[pl.ds(req * PAGE, PAGE)], page_sems, step - 1, ctx, target)))
-    near = (1, 2, 4, 3, 5, 6, 7)
     kv_copies = {0: own_kv}
     for group in near:
         kv_copies[group] = [
             start(remote(*kv_piece(group, part), gkv_sems, group * 2 + part, place(0, group)))
             for part in range(2)]
+    for group in near[:3]:
+        start(q_copy(group))
 
     for copy in page_copies:
         copy.wait_recv()
@@ -136,13 +139,12 @@
     for copy in group_pages:
         copy.wait_recv()
     prefixes = {1: pass_prefix(0, 1), 2: pass_prefix(0, 2)}
-    for group in near:
+    for group in near[3:]:
         start(q_copy(group))
 
-    def product(member, keys, queries_of=None):
-        queries_of = qbuf.at[member] if queries_of is None else queries_of
+    def product(member, keys):
         queries = jnp.concatenate(
-            [queries_of[:, g * HEAD_DIM:(g + 1) * HEAD_DIM] for g in range(GROUP_HEADS)], axis=0)
+            [qbuf[member, :, g * HEAD_DIM:(g + 1) * HEAD_DIM] for g in range(GROUP_HEADS)], axis=0)
         return lax.dot_general(queries, keys, (((1,), (1,)), ((), ())), preferred_element_type=jnp.float32)
 
     def weigh(scores, new, values):
@@ -180,24 +182,24 @@
         row = lax.broadcasted_iota(jnp.int32, (WIDE, 1), 0) % ROWS
         return jnp.where(token <= row, scores, LOW)
 
-    def near_keys(member, queries_of=None):
+    def near_keys(member):
         px, py, _ = spot(0, member)
         half = member // 4
-        held[0] = product(member, keys_of(near_kv, 0, half), queries_of)
+        held[0] = product(member, keys_of(near_kv, 0, half))
 
         @pl.when(px >= 2)
         def _():
-            held[1] = product(member, keys_of(near_kv, 0, 1 - half), queries_of)
+            held[1] = product(member, keys_of(near_kv, 0, 1 - half))
             begin(member, mask(held[0], 0, member), values_of(near_kv, 0, half))
-            held[0] = product(member, keys_of(near_kv, 1, half), queries_of)
+            held[0] = product(member, keys_of(near_kv, 1, half))
             absorb(member, held[1], values_of(near_kv, 0, 1 - half))
-            held[1] = product(member, keys_of(near_kv, 1, 1 - half), queries_of)
+            held[1] = product(member, keys_of(near_kv, 1, 1 - half))
             absorb(member, mask(held[0], 2, member), values_of(near_kv, 1, half))
             absorb(member, held[1], values_of(near_kv, 1, 1 - half))
 
         @pl.when((px < 2) & (py > 0))
         def _():
-            held[1] = product(member, keys_of(near_kv, 1, half), queries_of)
+            held[1] = product(member, keys_of(near_kv, 1, half))
             begin(member, mask(held[0], 0, member), values_of(near_kv, 0, half))
             absorb(member, mask(held[1], 2, member), values_of(near_kv, 1, half))
 
@@ -229,13 +231,26 @@
     prefixes[1].wait_recv()
     prefixes[3] = pass_prefix(1, 2)
     own_q.wait()
-    if COMPUTE:
-        near_keys(0, q_own)
-    qbuf[0] = q_own[...]
-    for group in near:
+    for group in near[:3]:
         q_copy(group).wait_recv()
-    if COMPUTE:
-        lax.fori_loop(1, MEMBERS, lambda member, _: (near_keys(member), 0)[1], 0)
+    qbuf[0] = q_first[0]
+    for group in near[:3]:
+        qbuf[group] = q_first[near.index(group) + 1]
+
+    def near_turn(turn, _):
+        @pl.when(turn == 4)
+        def _():
+            for group in near[3:]:
+                q_copy(group).wait_recv()
+                qbuf[group] = q_second[near.index(group) - 3]
+
+        late = turn // 4
+        member = (1 - late) * (turn + turn // 3) + late * (turn - (7 - turn) // 3)
+        if COMPUTE:
+            near_keys(member)
+        return 0
+
+    lax.fori_loop(0, MEMBERS, near_turn, 0)
 
     prefixes[2].wait_recv()
     prefixes[3].wait_recv()
@@ -327,7 +342,8 @@
         in_specs=[smem_spec, smem_spec, any_spec, any_spec, pl.BlockSpec(memory_space=vmem)],
         out_specs=any_spec,
         scratch_shapes=[
-            vmem((ROWS, Q_COLS), jnp.bfloat16),
+            vmem((4, ROWS, Q_COLS), jnp.bfloat16),
+            vmem((4, ROWS, Q_COLS), jnp.bfloat16),
             vmem((MEMBERS, ROWS, Q_COLS), jnp.bfloat16),
             vmem((SQUARE // 2, MEMBERS, ROWS, 2 * HEAD_DIM), jnp.bfloat16),
             vmem((SQUARE // 2, MEMBERS, ROWS, 2 * HEAD_DIM), jnp.bfloat16),

time: 111 us -> 97.6 us (0.88)
  the two profiles are of different devices: /device:TPU:6 before, /device:TPU:2 now
where the time goes in v3:
time: 97.6 us; the launch traced here: 96 us
  Pallas kernels  92 us (94%)
  other arithmetic  1.45 us (1%)
  local copies, waits for them, and re-layouts  1.32 us (1%)
    pallas_call x1, Pallas kernels, attend(): pl.pallas_call(functools.partial(kernel, room), out_shape=jax.ShapeDtypeS...  92 us

profile of v3, /device:TPU:2, one launch (start us, length us, event | category | flops | bytes accessed | tf_op | source)
XLA Modules:
  0.0 96.0 jit_solution(12778643841208085082)
XLA Ops:
  0.0 0.8 select_reduce_fusion
  0.8 0.6 reduce_max.9
  2.1 92.5 %conditional.1 = (bf16[1,128,8192]{2,1,0:T(8,128)(2,1)S(1)}) conditional(s32[]{:T(128)} %convert_element_type.3, (s32[256]{0:T(256)}, s32[256]{0:T(256)}, bf16[1,128,8192]{2,1,0:T(8,128)(2,1)}, bf16[1,128,2048]{2,1,0:T(8,128)(2,1)}, bf16[2,16,2048]{2,1,0:T(8,128)(2,1)}) %tuple.11, (s32[256]{0:T(256)}, s32[256]{0:T(256)}, ...), branch_computations={%region_2.3_spmd, %region_3.4_spmd} | conditional | flops 12000000000 | bytes 6000008 | solution.py:378
  2.3 92.0 %branch_1_fun.1 = bf16[1,128,8192]{2,1,0:T(8,128)(2,1)S(1)} custom-call(s32[256]{0:T(256)} %get-tuple-element.33.owner, s32[256]{0:T(256)} %get-tuple-element.34.fill, bf16[1,128,8192]{2,1,0:T(8,128)(2,1)} %get-tuple-element.46.q_hbm, bf16[1,128,2048]{2,1,0:T(8,128)(2,1)} %get-tuple-element.48.kv_hbm, bf16[2,16,2048]{2,1,0:T(8,128)(2,1)} %get-tuple-element.50.pages), custom_call_target="tpu_custom_call" | custom-call | flops 12000000000 | bytes 6000000 | tf_op jit(solution)/shard_map/cond/branch_1_fun/pallas_call | solution.py:339
  94.6 1.3 %copy.17 = bf16[1,128,8192]{2,1,0:T(8,128)(2,1)} copy(bf16[1,128,8192]{2,1,0:T(8,128)(2,1)S(1)} %get-tuple-element.38) | data formatting | bytes 4194304
